TPU v7x, 512 devices: a whole 4x4x16 slice. The times are simulated.
512 devices in a mesh: sect: 2 (over core), grp: 32 (over z_hi, x, y), seq: 8 (over z_lo).
Axes of the slice: x: 4, y: 4, z: 16 (z_hi: 2, z_lo: 8; z = z_hi * 8 + z_lo), core: 2. Of those that a mesh axis runs over, the one named last changes fastest.
Arguments:
- qkv_img: bfloat16 [32, 2048, 3, 2048], P('grp', ('sect', 'seq')), may hold values from -60 to 60
- img_seg: int32 [32, 2048], P('grp', ('sect', 'seq')), may hold values from 0 to 3, never falling along the last dimension, each value on 1 to 1024 neighbouring positions
- text_kv: bfloat16 [128, 2, 64, 2048], P('grp', None, None, ('sect', 'seq')), may hold values from -6 to 6
- txt_len: int32 [128], P('grp'), may hold values from 1 to 64
- req_slot: int32 [128], P('grp'), may hold values from 0 to 127, each once
Outputs:
- attn_out: bfloat16 [32, 2048, 2048], P('grp', ('sect', 'seq'))
Inputs may be any that keep to these rules, and one draw needn't show every extreme that they name: Request r goes to group req_slot[r] // 4 as its slot req_slot[r] % 4.
All inputs are finite; a program needn't handle non-finite values.
Results may differ from a plain program's by a relative error of at most 0.008.
Values may be sent and summed in bfloat16 or wider, within the bound.
A program may use at most 128 MiB of HBM per device.

v0:
```python
import jax
import jax.numpy as jnp
from jax import lax
from jax.sharding import PartitionSpec as P

HD = 128
REQ_G = 4


big_negative = -1e30


def attend_rows(query, keys, values, allowed):
    scale = 1.0 / query.shape[-1] ** 0.5
    scores = jnp.einsum("qd,kd->qk", query, keys, preferred_element_type=jnp.float32) * scale
    scores = jnp.where(allowed, scores, big_negative)
    top = jnp.max(scores, axis=1, keepdims=True)
    weights = jnp.where(allowed, jnp.exp(scores - top), 0.0)
    total = jnp.sum(weights, axis=1, keepdims=True)
    mixed = jnp.dot(weights.astype(jnp.bfloat16), values, preferred_element_type=jnp.float32)
    return (mixed / total).astype(jnp.bfloat16)


def local(qkv_img, img_seg, text_kv, txt_len, req_slot):
    group_index = lax.axis_index("grp")
    txt_tokens = text_kv.shape[2]
    wanted = group_index * REQ_G + lax.broadcasted_iota(jnp.int32, (REQ_G, 1), 0)
    empty_text = jnp.zeros((REQ_G,) + text_kv.shape[1:], jnp.float32)
    empty_lens = jnp.zeros((REQ_G,), jnp.int32)
    kv_piece = lax.all_gather(text_kv, "grp", axis=0, tiled=True)
    len_piece = lax.all_gather(txt_len, "grp", axis=0, tiled=True)
    slot_piece = lax.all_gather(req_slot, "grp", axis=0, tiled=True)
    chosen = slot_piece[None, :] == wanted
    picked = jnp.einsum(
        "jr,rstc->jstc", chosen.astype(jnp.bfloat16), kv_piece, preferred_element_type=jnp.float32
    )
    counts = jnp.sum(jnp.where(chosen, len_piece[None, :], 0), axis=1)
    lens = (empty_text, empty_lens)[1] + counts
    text_sel = picked.astype(jnp.bfloat16)
    token_pos = lax.broadcasted_iota(jnp.int32, (REQ_G, txt_tokens), 1)
    slot_ids = lax.broadcasted_iota(jnp.int32, (REQ_G, txt_tokens), 0)
    text_seg = jnp.where(token_pos < lens[:, None], slot_ids, -1).reshape(-1)
    text_count = REQ_G * txt_tokens
    spread = lax.all_to_all(qkv_img, ("sect", "seq"), split_axis=3, concat_axis=1, tiled=True)
    seg_full = lax.all_gather(img_seg, ("sect", "seq"), axis=1, tiled=True)[0]
    seq_len = spread.shape[1]
    key_seg = jnp.concatenate([seg_full, text_seg])
    block = min(512, seq_len)
    query = spread[0, :, 0, 0:HD]
    keys = jnp.concatenate(
        [spread[0, :, 1, 0:HD], text_sel[:, 0, :, 0:HD].reshape(text_count, HD)], 0
    )
    values = jnp.concatenate(
        [spread[0, :, 2, 0:HD], text_sel[:, 1, :, 0:HD].reshape(text_count, HD)], 0
    )

    def one_block(pair):
        block_query, block_seg = pair
        return attend_rows(block_query, keys, values, block_seg[:, None] == key_seg[None, :])

    result = lax.map(
        one_block,
        (query.reshape(seq_len // block, block, HD), seg_full.reshape(seq_len // block, block)),
    )
    outputs = result.reshape(seq_len, HD)
    joined = outputs[None]
    attn_out = lax.all_to_all(joined, ("sect", "seq"), split_axis=1, concat_axis=2, tiled=True)
    return attn_out


def solution(mesh):
    return jax.shard_map(
        local,
        mesh=mesh,
        in_specs=(
            P("grp", ("sect", "seq"), None, None),
            P("grp", ("sect", "seq")),
            P("grp", None, None, ("sect", "seq")),
            P("grp"),
            P("grp"),
        ),
        out_specs=P("grp", ("sect", "seq"), None),
        check_vma=False,
    )
```

profile of v0, /device:TPU:1, one launch (start us, length us, event | category | flops | bytes accessed | tf_op | source)
XLA Modules:
  0.0 306.2 jit_solution(14527738616499395432)
XLA Ops:
  7.3 4.2 %copy.25 = bf16[1,128,3,2048]{1,2,0,3:T(4,128)(2,1)} copy(bf16[1,128,3,2048]{3,1,2,0:T(8,128)(2,1)} %param.7) | data formatting | bytes 3145728 | tf_op args[0]
  11.4 14.0 %all-to-all-start = ((bf16[1,128,3,2048]{1,2,0,3:T(4,128)(2,1)}), bf16[1,128,3,2048]{1,2,0,3:T(4,128)(2,1)S(1)}, u32[]{:S(2)}, u32[]{:S(2)}) async-start(bf16[1,128,3,2048]{1,2,0,3:T(4,128)(2,1)} %copy.25), calls=%async_computation | async-start | bytes 4194304 | tf_op jit(solution)/shard_map/all_to_all | solution.py:44
  25.5 1.3 dynamic-slice
  27.8 47.2 %all-reduce.2 = (s32[128]{0:T(128)S(1)}, s32[128]{0:T(128)S(1)}) all-reduce(s32[128]{0:T(128)S(1)} %dynamic-update-slice.1, s32[128]{0:T(128)S(1)} %dynamic-update-slice), channel_id=1, replica_groups=mesh['sect'=2,'grp'=32,'seq'=8] {'grp'}, use_global_device_ids=true, to_apply=%add.1 | all-reduce | flops 256 | bytes 2048
  75.4 116.1 %all_gather.12 = s32[1,2048]{1,0:T(1,128)S(1)} all-gather(s32[1,128]{1,0:T(1,128)S(1)} %copy-done), channel_id=1, replica_groups=mesh['sect'=2,'grp'=32,'seq'=8] {'sect','seq'}, dimensions={1}, use_global_device_ids=true | all-gather | bytes 8704 | tf_op jit(solution)/shard_map/all_gather | solution.py:45
  192.6 2.4 copy.26
  195.0 1.5 slice_bitcast_fusion
  196.5 30.0 %all-gather.2.cloned.1.call-done = bf16[128,2,64,128]{3,2,1,0:T(8,128)(2,1)} async-done(((bf16[4,2,64,128]{3,2,1,0:T(8,128)(2,1)}), bf16[128,2,64,128]{3,2,1,0:T(8,128)(2,1)}) %all-gather.2.cloned.1.call-update) | async-done | bytes 4194320 | tf_op jit(solution)/shard_map/all_gather | solution.py:30
  226.4 4.5 %fusion.22 = bf16[4,2,64,128]{3,0,2,1:T(4,128)(2,1)S(1)} fusion(bf16[128,2,64,128]{3,2,1,0:T(8,128)(2,1)} %all-gather.2.cloned.1.call-done, s32[128]{0:T(128)S(1)} %get-tuple-element.58, s32[4]{0:T(128)S(1)} %iota_add_fusion), kind=kOutput, calls=%fused_computation.17 | convolution fusion | flops 16843264 | bytes 4325904 | tf_op jit(solution)/shard_map/jr,rstc->jstc/dot_general | solution.py:34
  231.1 12.8 %while.10 = (s32[]{:T(128)}, bf16[4,512,128]{2,1,0:T(8,128)(2,1)S(1)}, s32[4,512]{1,0:T(4,128)S(1)}, s32[2304]{0:T(1024)S(1)}, bf16[4,512,128]{2,1,0:T(8,128)(2,...) while((s32[]{:T(128)}, bf16[4,512,128]{2,1,0:T(8,128)(2,1)S(1)}, ...), condition=%wide.region_4.5_spmd, body=%wide.region_1.4_spmd.sunk | while | flops 618265600 | bytes 15651937 | solution.py:61
  231.2 1.0 fusion.41
  232.2 1.1 fusion.42
  233.3 1.0 fusion.43
  235.4 1.1 fusion.42
  236.5 1.0 fusion.43
  237.5 1.0 fusion.41
  238.6 1.1 fusion.42
  239.6 1.0 fusion.43
  240.7 1.0 fusion.41
  241.8 1.1 fusion.42
  242.8 1.0 fusion.43
  243.9 8.1 %copy.40 = bf16[1,2048,128]{2,0,1:T(2,128)(2,1)S(1)} copy(bf16[1,2048,128]{2,1,0:T(8,128)(2,1)S(1)} %bitcast.55) | data formatting | bytes 1048576 | tf_op jit(solution)/shard_map/broadcast_in_dim;reshape | solution.py:66
  252.6 11.7 %reduce.4 = bf16[2048,128]{1,0:T(8,128)(2,1)S(1)} reduce(bf16[2048,1,128]{2,1,0:T(2,128)(2,1)S(1)} %bitcast.52, bf16[]{:T(256)} %broadcast.29), dimensions={1}, to_apply=%bitcast.38.reduce_sub_computation | reduce | bytes 1048578
  264.4 33.1 %all_to_all.36 = bf16[16,2,8192]{2,1,0:T(2,128)(2,1)S(1)} all-to-all(bf16[16,2,8192]{2,1,0:T(2,128)(2,1)S(1)} %reshape.40), channel_id=1, replica_groups=mesh['sect'=2,'grp'=32,'seq'=8] {'sect','seq'}, dimensions={0} | all-to-all | bytes 1048576 | tf_op jit(solution)/shard_map/all_to_all | solution.py:67
  (37 shorter events, 6.4 us)
Async XLA Ops:
  6.5 20.8 %copy-start.1 = (s32[4]{0:T(128)S(1)}, s32[4]{0:T(128)}, u32[]{:S(2)}) copy-start(s32[4]{0:T(128)} %param.11) | copy-start | bytes 52
  6.5 21.1 %copy-start.2 = (s32[4]{0:T(128)S(1)}, s32[4]{0:T(128)}, u32[]{:S(2)}) copy-start(s32[4]{0:T(128)} %param.10) | copy-start | bytes 52
  6.5 68.8 %copy-start = (s32[1,128]{1,0:T(1,128)S(1)}, s32[1,128]{1,0:T(1,128)}, u32[]{:S(2)}) copy-start(s32[1,128]{1,0:T(1,128)} %param.8) | copy-start | bytes 1540
  6.5 219.9 %all-gather.2.cloned.1.call-start = ((), (), s32[]{:S(2)}) async-start(), calls=%async_computation.2 | async-start | bytes 4325376 | tf_op jit(solution)/shard_map/all_gather | solution.py:30
  11.4 181.2 %all-to-all-start = ((bf16[1,128,3,2048]{1,2,0,3:T(4,128)(2,1)}), bf16[1,128,3,2048]{1,2,0,3:T(4,128)(2,1)S(1)}, u32[]{:S(2)}, u32[]{:S(2)}) async-start(bf16[1,128,3,2048]{1,2,0,3:T(4,128)(2,1)} %copy.25), calls=%async_computation | async-start | bytes 4194304 | tf_op jit(solution)/shard_map/all_to_all | solution.py:44
Sparse Core Ops, SparseCore 0:
  11.8 214.6 all-gather.1
where the time goes:
time: 307 us; the launch traced here: 306 us
  blocking collectives  196 us (64%)
  waiting for transfers between devices  30.7 us (10%)
  local copies, waits for them, and re-layouts  21.1 us (7%)
  other arithmetic  17 us (6%)
  between operations  14.1 us (5%)
  starting transfers between devices  14 us (5%)
  matrix products  12.8 us (4%)
    all_gather x1, blocking collectives, local(): seg_full = lax.all_gather(img_seg, ('sect', 'seq'), axis=1, tiled=True)[0]  116 us
    unnamed x1, blocking collectives  47.2 us
    all_to_all x1, blocking collectives, local(): lax.all_to_all(joined, ('sect', 'seq'), split_axis=1, concat_axis=2, tile...  33.1 us
    all_gather x1, waiting for transfers between devices, local(): kv_piece = lax.all_gather(text_kv, 'grp', axis=0, tiled=True)  30 us
    all_to_all x1, starting transfers between devices, local(): lax.all_to_all(qkv_img, ('sect', 'seq'), split_axis=3, concat_axis=1, til...  14 us
    unnamed x1, other arithmetic  11.7 us
    another operation x1, local copies, waits for them, and re-layouts, local(): joined = outputs[None]  8.14 us
    unnamed x16, local copies, waits for them, and re-layouts  7.14 us
  transfers between devices with their start and end apart: 2, of which 1 were waited for; matrix products, arithmetic and copies ran while one was open for 4% of the time, Pallas kernels for 0%

commit v1 on v0

v1 whole, which is shorter than its diff:
```python
import functools

import jax
import jax.numpy as jnp
from jax import lax
from jax.experimental import pallas as pl
from jax.experimental.pallas import tpu as pltpu
from jax.sharding import PartitionSpec as P

HD = 128
REQ_G = 4
GRID = (2, 4, 4)
MESH = pl.DeviceIdType.MESH

FAR = -2097152.0
LOG2E = 1.4426950408889634


def kernel(
    dims,
    slot_ref, len_ref, x_ref, seg_ref, text_ref,
    out_ref,
    kv, k_mask, qb, q_mask, ob, landed, score, prob, seg_send, segs, meta_send, meta_y, meta_sm, text_y, text_xs, text_x, meta_xs, meta_x, meta_xm,
    local_sem, seg_ss, seg_rs, kv_ss, kv_rs, q_ss, q_rs, o_ss, o_rs,
    tz_s, tz_r, ty_s, ty_r, tx_s, tx_r,
):
    n_seq, n_sect, n_hi, n_x, n_y = dims
    blocks = n_seq * n_sect
    tok = x_ref.shape[1]
    img = blocks * tok
    txt = text_ref.shape[2]
    keys = img + REQ_G * txt
    sect, grp, seq = lax.axis_index("sect"), lax.axis_index("grp"), lax.axis_index("seq")
    z_hi, gx, gy = lax.div(grp, n_x * n_y), lax.rem(lax.div(grp, n_y), n_x), lax.rem(grp, n_y)

    def chip_at(d):
        total, unit = 0, 1
        while unit < n_seq:
            total = total + unit * lax.rem(lax.div(seq, unit) + lax.div(d, unit), 2)
            unit *= 2
        return total

    def core_at(c):
        return lax.rem(sect + c, n_sect)

    def columns(d, c):
        return pl.ds(pl.multiple_of((core_at(c) * n_seq + chip_at(d)) * HD, HD), HD)

    def peer(d, c):
        return {"sect": core_at(c), "grp": grp, "seq": chip_at(d)}

    def member(hi, x, y):
        return (hi * n_x + x) * n_y + y

    def peer_group(hi, x, y):
        return {"sect": sect, "grp": member(hi, x, y), "seq": seq}

    def far(k):
        return peer_group(lax.rem(z_hi + k, n_hi), gx, gy)

    def along_y(k):
        return peer_group(z_hi, gx, lax.rem(gy + k, n_y))

    def along_x(k):
        return peer_group(z_hi, lax.rem(gx + k, n_x), gy)

    zero = jnp.int32(0)

    def each_peer(body):
        @pl.loop(1, n_seq)
        def _(i):
            for c in range(n_sect):
                body(n_seq - i, c)

        for c in range(1, n_sect):
            body(zero, c)

    lane = lax.broadcasted_iota(jnp.int32, (8, 128), 1)
    meta = jnp.zeros((8, 128), jnp.int32)
    for r in range(REQ_G):
        meta = jnp.where(lane == r, slot_ref[r], meta)
        meta = jnp.where(lane == REQ_G + r, len_ref[r], meta)
    meta_send[...] = meta
    meta_y[0, 0] = meta
    seg_send[...] = jnp.broadcast_to(seg_ref[...], (8, tok))
    segs[0] = jnp.broadcast_to(seg_ref[...], (8, tok))

    barrier = pltpu.get_barrier_semaphore()

    def greet(device):
        pl.semaphore_signal(barrier, inc=1, device_id=device, device_id_type=MESH)

    each_peer(lambda d, c: greet(peer(d, c)))
    greet(far(1))
    for k in range(1, n_y):
        greet(along_y(k))
    for k in range(1, n_x):
        greet(along_x(k))
    pl.semaphore_wait(barrier, blocks - 1 + 1 + (n_y - 1) + (n_x - 1))

    def remote(src, dst, ss, rs, device):
        return pltpu.make_async_remote_copy(
            src_ref=src, dst_ref=dst, send_sem=ss, recv_sem=rs, device_id=device, device_id_type=MESH)

    def hop_z():
        return (
            remote(meta_send, meta_y.at[0, 1], tz_s.at[0], tz_r.at[0], far(1)),
            remote(text_ref, text_y.at[0, 1], tz_s.at[1], tz_r.at[1], far(1)),
        )

    for copy in hop_z():
        copy.start()

    def move_seg(d, c):
        at = d * n_sect + c
        return remote(seg_send, segs.at[at], seg_ss.at[at], seg_rs.at[at], peer(d, c))

    def move_kv(d, c):
        at = d * n_sect + c
        return remote(x_ref.at[pl.ds(1, 2), :, columns(d, c)], kv.at[at], kv_ss.at[at], kv_rs.at[at], peer(d, c))

    def move_q(d, c):
        at = d * n_sect + c
        return remote(x_ref.at[0, :, columns(d, c)], qb.at[at], q_ss.at[at], q_rs.at[at], peer(d, c))

    def move_o(d, c):
        at = d * n_sect + c
        return remote(ob.at[at], landed.at[at], o_ss.at[at], o_rs.at[at], peer(d, c))

    each_peer(lambda d, c: move_seg(d, c).start())
    each_peer(lambda d, c: move_kv(d, c).start())

    own_text = pltpu.make_async_copy(text_ref, text_y.at[0, 0], local_sem.at[0])
    own_text.start()
    own_kv = pltpu.make_async_copy(x_ref.at[pl.ds(1, 2), :, columns(zero, 0)], kv.at[0], local_sem.at[1])
    own_kv.start()
    own_q = pltpu.make_async_copy(x_ref.at[0, :, columns(zero, 0)], qb.at[0], local_sem.at[2])
    own_q.start()
    each_peer(lambda d, c: move_q(d, c).start())

    each_peer(lambda d, c: move_seg(d, c).wait())

    spot = lax.broadcasted_iota(jnp.int32, (tok, HD), 1)

    @pl.loop(0, blocks)
    def _(b):
        row = segs[b]
        across = jnp.broadcast_to(row[0:1, :], (tok, tok))
        down = jnp.transpose(across)
        q_mask[b] = jnp.where(spot == down, 1.0, 0.0).astype(jnp.bfloat16)
        k_mask[b] = jnp.where((spot < REQ_G) & (spot != down), FAR, 0.0).astype(jnp.bfloat16)

    own_text.wait()
    for copy in hop_z():
        copy.wait()

    def hop_y(k):
        return (
            remote(meta_y.at[0], meta_y.at[k], ty_s.at[0, k], ty_r.at[0, k], along_y(k)),
            remote(text_y.at[0], text_y.at[k], ty_s.at[1, k], ty_r.at[1, k], along_y(k)),
        )

    for k in range(1, n_y):
        for copy in hop_y(k):
            copy.start()
    for k in range(1, n_y):
        for copy in hop_y(k):
            copy.wait()

    to_scalars = pltpu.make_async_copy(meta_y, meta_sm, local_sem.at[3])
    to_scalars.start()
    to_scalars.wait()

    for k in range(n_x):
        first = member(z_hi, lax.rem(gx + k, n_x), gy) * REQ_G
        lens = jnp.zeros((8, 128), jnp.int32)
        for j in range(REQ_G):
            def look(s, carry):
                at_y, at_hi, at_r, count = carry
                sy, sh, sr = lax.div(s, n_hi * REQ_G), lax.rem(lax.div(s, REQ_G), n_hi), lax.rem(s, REQ_G)
                hit = meta_sm[sy, sh, 0, sr] == first + j
                return (
                    jnp.where(hit, sy, at_y),
                    jnp.where(hit, sh, at_hi),
                    jnp.where(hit, sr, at_r),
                    jnp.where(hit, meta_sm[sy, sh, 0, REQ_G + sr], count),
                )

            at_y, at_hi, at_r, count = lax.fori_loop(0, n_y * n_hi * REQ_G, look, (zero, zero, zero, zero))
            text_xs[k, j] = text_y[at_y, at_hi, at_r]
            lens = jnp.where(lane == j, count, lens)
        meta_xs[k] = lens

    def hop_x(k):
        return (
            remote(meta_xs.at[k], meta_x.at[k], tx_s.at[0, k], tx_r.at[0, k], along_x(k)),
            remote(text_xs.at[k], text_x.at[k], tx_s.at[1, k], tx_r.at[1, k], along_x(k)),
        )

    for k in range(1, n_x):
        for copy in hop_x(k):
            copy.start()
    for k in range(1, n_x):
        for copy in hop_x(k):
            copy.wait()
    text_x[0] = text_xs[0]
    meta_x[0] = meta_xs[0]

    to_scalars = pltpu.make_async_copy(meta_x, meta_xm, local_sem.at[4])
    to_scalars.start()
    to_scalars.wait()

    own_kv.wait()
    own_q.wait()
    each_peer(lambda d, c: move_kv(d, c).wait())

    place = lax.broadcasted_iota(jnp.int32, (txt, HD), 0)
    spot_t = lax.broadcasted_iota(jnp.int32, (txt, HD), 1)
    for j in range(REQ_G):
        at_x, count = zero, zero
        for k in range(n_x):
            here = meta_xm[k, 0, j]
            at_x = jnp.where(here > 0, k, at_x)
            count = jnp.where(here > 0, here, count)
        block, part = blocks + (j * txt) // tok, pl.ds((j * txt) % tok, txt)
        kv[block, 0, part] = text_x[at_x, j, 0]
        kv[block, 1, part] = text_x[at_x, j, 1]
        live = (spot_t == j) & (place < count)
        k_mask[block, part] = jnp.where((spot_t < REQ_G) & ~live, FAR, 0.0).astype(jnp.bfloat16)

    factor = LOG2E / HD ** 0.5
    pair = n_sect * tok

    def attend(d):
        both = pl.ds(d * n_sect, n_sect)
        score[...] = lax.dot_general(
            jnp.concatenate([qb[both].reshape(pair, HD), q_mask[both].reshape(pair, HD)], axis=1),
            jnp.concatenate([kv[:, 0].reshape(keys, HD), k_mask[...].reshape(keys, HD)], axis=1),
            (((1,), (1,)), ((), ())), preferred_element_type=jnp.float32)
        top = jnp.max(score[...], axis=1, keepdims=True)
        prob[...] = jnp.exp2((score[...] - top) * factor).astype(jnp.bfloat16)
        mixed = jnp.dot(
            prob[...], jnp.concatenate([kv[:, 1].reshape(keys, HD), jnp.ones((keys, HD), jnp.bfloat16)], axis=1),
            preferred_element_type=jnp.float32)
        ob[both] = (mixed[:, :HD] / mixed[:, HD:]).astype(jnp.bfloat16).reshape(n_sect, tok, HD)

    for c in range(1, n_sect):
        move_q(zero, c).wait()
    attend(0)
    for c in range(1, n_sect):
        move_o(zero, c).start()

    @pl.loop(1, n_seq)
    def _(i):
        d = n_seq - i
        for c in range(n_sect):
            move_q(d, c).wait()
        attend(d)
        for c in range(n_sect):
            move_o(d, c).start()

    out_ref[:, columns(zero, 0)] = ob[0]

    def finish(d, c):
        move_o(d, c).wait()
        out_ref[:, columns(d, c)] = landed[d * n_sect + c]

    each_peer(finish)


def local(mesh, qkv_img, img_seg, text_kv, txt_len, req_slot):
    n_seq, n_sect = mesh.shape["seq"], mesh.shape["sect"]
    n_hi, n_x, n_y = GRID
    blocks = n_seq * n_sect
    tok, width = qkv_img.shape[1], qkv_img.shape[3]
    txt = text_kv.shape[2]
    keys = blocks * tok + REQ_G * txt
    x = jnp.transpose(qkv_img[0], (1, 0, 2))
    dma = pltpu.SemaphoreType.DMA
    bf16, i32 = jnp.bfloat16, jnp.int32
    out = pl.pallas_call(
        functools.partial(kernel, (n_seq, n_sect, n_hi, n_x, n_y)),
        out_shape=jax.ShapeDtypeStruct((tok, width), bf16),
        in_specs=[
            pl.BlockSpec(memory_space=pltpu.SMEM),
            pl.BlockSpec(memory_space=pltpu.SMEM),
            pl.BlockSpec(memory_space=pl.ANY),
            pl.BlockSpec(memory_space=pltpu.VMEM),
            pl.BlockSpec(memory_space=pl.ANY),
        ],
        out_specs=pl.BlockSpec(memory_space=pltpu.VMEM),
        scratch_shapes=[
            pltpu.VMEM((keys // tok, 2, tok, HD), bf16),
            pltpu.VMEM((keys // tok, tok, HD), bf16),
            pltpu.VMEM((blocks, tok, HD), bf16),
            pltpu.VMEM((blocks, tok, HD), bf16),
            pltpu.VMEM((blocks, tok, HD), bf16),
            pltpu.VMEM((blocks, tok, HD), bf16),
            pltpu.VMEM((n_sect * tok, keys), jnp.float32),
            pltpu.VMEM((n_sect * tok, keys), bf16),
            pltpu.VMEM((8, tok), i32),
            pltpu.VMEM((blocks, 8, tok), i32),
            pltpu.VMEM((8, 128), i32),
            pltpu.VMEM((n_y, n_hi, 8, 128), i32),
            pltpu.SMEM((n_y, n_hi, 8, 128), i32),
            pltpu.VMEM((n_y, n_hi, REQ_G, 2, txt, HD), bf16),
            pltpu.VMEM((n_x, REQ_G, 2, txt, HD), bf16),
            pltpu.VMEM((n_x, REQ_G, 2, txt, HD), bf16),
            pltpu.VMEM((n_x, 8, 128), i32),
            pltpu.VMEM((n_x, 8, 128), i32),
            pltpu.SMEM((n_x, 8, 128), i32),
            dma((5,)),
            dma((blocks,)), dma((blocks,)),
            dma((blocks,)), dma((blocks,)),
            dma((blocks,)), dma((blocks,)),
            dma((blocks,)), dma((blocks,)),
            dma((2,)), dma((2,)),
            dma((2, n_y)), dma((2, n_y)),
            dma((2, n_x)), dma((2, n_x)),
        ],
        compiler_params=pltpu.CompilerParams(
            collective_id=0, has_side_effects=True, vmem_limit_bytes=40 * 1024 * 1024),
        name="routed_attention",
    )(req_slot, txt_len, x, img_seg, text_kv)
    return out[None]


def solution(mesh):
    return jax.shard_map(
        functools.partial(local, mesh),
        mesh=mesh,
        in_specs=(
            P("grp", ("sect", "seq"), None, None),
            P("grp", ("sect", "seq")),
            P("grp", None, None, ("sect", "seq")),
            P("grp"),
            P("grp"),
        ),
        out_specs=P("grp", ("sect", "seq"), None),
        check_vma=False,
    )
```

time: 307 us -> 130 us (0.42)
  blocking collectives: 196 us -> 0 us
  Pallas kernels: 0 us -> 125 us
  waiting for transfers between devices: 30.7 us -> 0 us
  other arithmetic: 17 us -> 0 us
  local copies, waits for them, and re-layouts: 21.1 us -> 5.07 us
  between operations: 14.1 us -> 0.01 us
  starting transfers between devices: 14 us -> 0 us
  matrix products: 12.8 us -> 0 us
    pallas_call x0 -> x1, Pallas kernels: none -> 125 us  [local(): pl.pallas_call(functools.partial(kernel, (n_seq, n_sect, n_hi, n_x, n_y))...]
    all_gather x1 -> x0, blocking collectives: 116 us -> none  [local(): seg_full = lax.all_gather(img_seg, ('sect', 'seq'), axis=1, tiled=True)[0]]
    unnamed x1 -> x0, blocking collectives: 47.2 us -> none
    all_to_all x1 -> x0, blocking collectives: 33.1 us -> none  [local(): lax.all_to_all(joined, ('sect', 'seq'), split_axis=1, concat_axis=2, tile...]
    all_gather x1 -> x0, waiting for transfers between devices: 30 us -> none  [local(): kv_piece = lax.all_gather(text_kv, 'grp', axis=0, tiled=True)]
    all_to_all x1 -> x0, starting transfers between devices: 14 us -> none  [local(): lax.all_to_all(qkv_img, ('sect', 'seq'), split_axis=3, concat_axis=1, til...]
    dot_general x9 -> x0, matrix products: 12.8 us -> none  [the longest x1 4.51 us: local(): jnp.einsum('jr,rstc->jstc', chosen.astype(jnp.bfloat16), kv_piece, prefer...]
    unnamed x1 -> x0, other arithmetic: 11.7 us -> none
  transfers between devices with their start and end apart: 2 -> 0, of which waited for: 1 -> 0; matrix products, arithmetic and copies ran while one was open for 4% -> 0% of each run, Pallas kernels for 0% -> 0%
where the time goes in v1:
time: 130 us
  Pallas kernels  125 us (96%)
  local copies, waits for them, and re-layouts  5.07 us (4%)
    pallas_call x1, Pallas kernels, local(): pl.pallas_call(functools.partial(kernel, (n_seq, n_sect, n_hi, n_x, n_y))...  125 us
    unnamed x11, local copies, waits for them, and re-layouts  5.07 us

profile of v1, /device:TPU:1, one launch (start us, length us, event | category | flops | bytes accessed | tf_op | source)
XLA Modules:
  0.0 129.8 jit_solution(6220482269202587690)
XLA Ops:
  0.0 0.0 copy-start
  0.0 1.4 %copy-done = bf16[1,128,3,2048]{3,1,2,0:T(8,128)(2,1)S(1)} copy-done((bf16[1,128,3,2048]{3,1,2,0:T(8,128)(2,1)S(1)}, bf16[1,128,3,2048]{3,1,2,0:T(8,128)(2,1)}, u32[]{:S(2)}) %copy-start) | copy-done | bytes 1572888
  1.4 0.0 copy-start.1
  1.4 0.9 copy-done.1
  2.3 0.0 copy-start.2
  2.3 0.7 copy-done.2
  3.0 0.0 copy-start.3
  3.0 0.7 copy-done.3
  3.6 0.0 copy-start.4
  3.6 0.7 copy-done.4
  4.3 124.7 %routed_attention.1 = bf16[128,2048]{1,0:T(8,128)(2,1)S(1)} custom-call(s32[4]{0:T(128)S(1)} %copy-done.2, s32[4]{0:T(128)S(1)} %copy-done.3, bf16[3,128,2048]{2,1,0:T(8,128)(2,1)S(1)} %bitcast.5, s32[1,128]{1,0:T(1,128)S(1)} %copy-done.4, bf16[4,2,64,128]{3,2,1,0:T(8,128)(2,1)S(1)} %copy-done.1), custom_call_target="tpu_custom_call" | custom-call | tf_op jit(solution)/shard_map/routed_attention/pallas_call | solution.py:281
  129.0 0.8 copy.7
Async XLA Ops:
  0.0 1.4 %copy-start = (bf16[1,128,3,2048]{3,1,2,0:T(8,128)(2,1)S(1)}, bf16[1,128,3,2048]{3,1,2,0:T(8,128)(2,1)}, u32[]{:S(2)}) copy-start(bf16[1,128,3,2048]{3,1,2,0:T(8,128)(2,1)} %param.5) | copy-start | bytes 4718596
  1.4 0.9 copy-start.1
  2.3 0.7 copy-start.2
  3.0 0.7 copy-start.3
  3.6 0.7 copy-start.4

commit v2 on v1

v2 whole, which is shorter than its diff:
```python
import functools

import jax
import jax.numpy as jnp
from jax import lax
from jax.experimental import pallas as pl
from jax.experimental.pallas import tpu as pltpu
from jax.sharding import PartitionSpec as P

HD = 128
REQ_G = 4
GRID = (2, 4, 4)
MESH = pl.DeviceIdType.MESH

FAR = -2097152.0
LOG2E = 1.4426950408889634


def kernel(
    dims,
    slot_ref, len_ref, x_ref, seg_ref, text_ref,
    out_ref,
    kv, k_mask, qb, q_mask, ob, landed, score, prob, seg_send, segs,
    text_in, text_y, text_xs, text_x, text_far, text_own,
    meta_send, meta_in, meta_y, picks, meta_xs, meta_x, meta_far, meta_own,
    meta_sm, picks_sm, meta_xm, meta_own_sm, slots, counts, seg_row,
    local_sem, seg_ss, seg_rs, kv_ss, kv_rs, q_ss, q_rs, o_ss, o_rs,
    ta_s, ta_r, tb_s, tb_r, ty_s, ty_r, tx_s, tx_r, tc_s, tc_r,
):
    n_seq, n_sect, n_hi, n_x, n_y = dims
    blocks = n_seq * n_sect
    tok = x_ref.shape[1]
    img = blocks * tok
    txt = text_ref.shape[2]
    keys = img + REQ_G * txt
    sect, grp, seq = lax.axis_index("sect"), lax.axis_index("grp"), lax.axis_index("seq")
    z_hi, gx, gy = lax.div(grp, n_x * n_y), lax.rem(lax.div(grp, n_y), n_x), lax.rem(grp, n_y)

    def chip_at(d):
        total, unit = 0, 1
        while unit < n_seq:
            bit = (d // unit) % 2 if isinstance(d, int) else lax.div(d, unit)
            total = total + unit * lax.rem(lax.div(seq, unit) + bit, 2)
            unit *= 2
        return total

    def core_at(c):
        return lax.rem(sect + c, n_sect)

    def columns(d, c):
        chip = chip_at(d)
        head = core_at(c) * n_seq + chip + z_hi * (n_seq - 1 - 2 * chip)
        return pl.ds(pl.multiple_of(head * HD, HD), HD)

    def peer(d, c):
        return {"sect": core_at(c), "grp": grp, "seq": chip_at(d)}

    def member(hi, x, y):
        return (hi * n_x + x) * n_y + y

    far = {"sect": sect, "grp": member(n_hi - 1 - z_hi, gx, gy), "seq": n_seq - 1 - seq}

    def along_y(k):
        return {"sect": sect, "grp": member(z_hi, gx, lax.rem(gy + k, n_y)), "seq": seq}

    def along_x(k):
        return {"sect": sect, "grp": member(z_hi, lax.rem(gx + k, n_x), gy), "seq": seq}

    lower, upper = z_hi == 0, z_hi == 1

    def nth(i):
        return n_seq // 2 + (2 * (i % 2) - 1) * (i // 2) if isinstance(i, int) else (
            n_seq // 2 + (2 * lax.rem(i, 2) - 1) * lax.div(i, 2))

    order = [(nth(i), c) for i in range(1, n_seq) for c in range(n_sect)] + [(0, c) for c in range(1, n_sect)]

    def some(places, body):
        for d, c in places:
            body(d, c)

    def each_peer(body):
        @pl.loop(1, n_seq)
        def _(i):
            for c in range(n_sect):
                body(nth(i), c)

        for c in range(1, n_sect):
            body(0, c)

    small = (
        pltpu.make_async_copy(slot_ref, slots, local_sem.at[5]),
        pltpu.make_async_copy(len_ref, counts, local_sem.at[6]),
        pltpu.make_async_copy(seg_ref, seg_row, local_sem.at[7]),
    )
    for copy in small:
        copy.start()

    barrier = pltpu.get_barrier_semaphore()

    def greet(device):
        pl.semaphore_signal(barrier, inc=1, device_id=device, device_id_type=MESH)

    each_peer(lambda d, c: greet(peer(d, c)))

    @pl.when(lower)
    def _():
        for k in range(1, n_y):
            greet(along_y(k))
        for k in range(1, n_x):
            greet(along_x(k))

    for copy in small:
        copy.wait()
    lane = lax.broadcasted_iota(jnp.int32, (8, 128), 1)
    meta = jnp.zeros((8, 128), jnp.int32)
    for r in range(REQ_G):
        meta = jnp.where(lane == r, slots[r], meta)
        meta = jnp.where(lane == REQ_G + r, counts[r], meta)
    meta_send[...] = meta
    seg_send[...] = jnp.broadcast_to(seg_row[...], (8, tok))
    segs[0] = jnp.broadcast_to(seg_row[...], (8, tok))

    @pl.when(lower)
    def _():
        pl.semaphore_wait(barrier, blocks - 1 + n_y - 1 + n_x - 1)
        greet(far)

    @pl.when(upper)
    def _():
        pl.semaphore_wait(barrier, blocks - 1 + 1)
        greet(far)

    def remote(src, dst, ss, rs, device):
        return pltpu.make_async_remote_copy(
            src_ref=src, dst_ref=dst, send_sem=ss, recv_sem=rs, device_id=device, device_id_type=MESH)

    def start(copies):
        for copy in copies:
            copy.start()

    def wait(copies):
        for copy in copies:
            copy.wait()

    def hop_mirror():
        mate = peer(n_seq - 1, 0)
        return (
            remote(meta_send, meta_in, ta_s.at[0], ta_r.at[0], mate),
            remote(text_ref, text_in, ta_s.at[1], ta_r.at[1], mate),
        )

    def requests(half, k):
        return pl.ds((half * n_y + k) * REQ_G, REQ_G)

    def hop_down():
        return (
            remote(meta_in, meta_y.at[n_y], tb_s.at[0], tb_r.at[0], far),
            remote(text_in, text_y.at[requests(1, 0)], tb_s.at[1], tb_r.at[1], far),
        )

    def hop_y(half, k):
        meta_src = meta_y.at[n_y] if half else meta_send
        text_src = text_y.at[requests(1, 0)] if half else text_ref
        return (
            remote(meta_src, meta_y.at[half * n_y + k], ty_s.at[0, half, k], ty_r.at[0, half, k], along_y(k)),
            remote(text_src, text_y.at[requests(half, k)], ty_s.at[1, half, k], ty_r.at[1, half, k], along_y(k)),
        )

    def hop_x(k):
        return (
            remote(meta_xs, meta_x.at[k], tx_s.at[0, k], tx_r.at[0, k], along_x(k)),
            remote(text_xs.at[k], text_x.at[k], tx_s.at[1, k], tx_r.at[1, k], along_x(k)),
        )

    def hop_up():
        return (
            remote(meta_far, meta_own, tc_s.at[0], tc_r.at[0], far),
            remote(text_far, text_own, tc_s.at[1], tc_r.at[1], far),
        )

    def move_seg(d, c):
        at = d * n_sect + c
        return remote(seg_send, segs.at[at], seg_ss.at[at], seg_rs.at[at], peer(d, c))

    def move_kv(d, c):
        at = d * n_sect + c
        return remote(x_ref.at[pl.ds(1, 2), :, columns(d, c)], kv.at[at], kv_ss.at[at], kv_rs.at[at], peer(d, c))

    def move_q(d, c):
        at = d * n_sect + c
        return remote(x_ref.at[0, :, columns(d, c)], qb.at[at], q_ss.at[at], q_rs.at[at], peer(d, c))

    def move_o(d, c):
        at = d * n_sect + c
        return remote(ob.at[at], landed.at[at], o_ss.at[at], o_rs.at[at], peer(d, c))

    def send_kv(d, c):
        move_kv(d, c).start()

    def send_q(d, c):
        move_q(d, c).start()

    n1, n2 = 2 * n_sect, 5 * n_sect

    @pl.when(upper)
    def _():
        start(hop_mirror())

    each_peer(lambda d, c: move_seg(d, c).start())

    @pl.when(lower)
    def _():
        for k in range(1, n_y):
            start(hop_y(0, k))

    some(order[:n1], send_kv)

    own_text = pltpu.make_async_copy(text_ref, text_y.at[requests(0, 0)], local_sem.at[0])
    own_text.start()
    own_kv = pltpu.make_async_copy(x_ref.at[pl.ds(1, 2), :, columns(0, 0)], kv.at[0], local_sem.at[1])
    own_kv.start()
    own_q = pltpu.make_async_copy(x_ref.at[0, :, columns(0, 0)], qb.at[0], local_sem.at[2])
    own_q.start()
    meta_y[0] = meta

    @pl.when(upper)
    def _():
        wait(hop_mirror())
        start(hop_down())

    some(order[n1:n2], send_kv)

    each_peer(lambda d, c: move_seg(d, c).wait())

    spot = lax.broadcasted_iota(jnp.int32, (tok, HD), 1)

    @pl.loop(0, blocks)
    def _(b):
        row = segs[b]
        across = jnp.broadcast_to(row[0:1, :], (tok, tok))
        down = jnp.transpose(across)
        q_mask[b] = jnp.where(spot == down, 1.0, 0.0).astype(jnp.bfloat16)
        k_mask[b] = jnp.where((spot < REQ_G) & (spot != down), FAR, 0.0).astype(jnp.bfloat16)

    @pl.when(lower)
    def _():
        for copy in hop_down():
            copy.wait_recv()
        for k in range(1, n_y):
            start(hop_y(1, k))

    @pl.when(upper)
    def _():
        for copy in hop_down():
            copy.wait_send()

    some(order[n2:], send_kv)
    own_text.wait()

    @pl.when(lower)
    def _():
        for half in range(n_hi):
            for k in range(1, n_y):
                wait(hop_y(half, k))
        to_scalars = pltpu.make_async_copy(meta_y, meta_sm, local_sem.at[3])
        to_scalars.start()
        to_scalars.wait()
        per_x = n_hi * REQ_G
        to_x = lax.rem(gx + lax.div(lane, per_x), n_x)
        to_hi = lax.rem(lax.div(lane, REQ_G), n_hi)
        wanted = member(to_hi, to_x, gy) * REQ_G + lax.rem(lane, REQ_G)
        wanted = jnp.where(lane < n_x * per_x, wanted, -1)
        at, lens = jnp.zeros((8, 128), jnp.int32), jnp.zeros((8, 128), jnp.int32)
        for b in range(n_hi * n_y):
            for r in range(REQ_G):
                hit = wanted == meta_sm[b, 0, r]
                at = jnp.where(hit, b * REQ_G + r, at)
                lens = jnp.where(hit, meta_sm[b, 0, REQ_G + r], lens)
        picks[...] = at
        meta_xs[...] = lens
        to_scalars = pltpu.make_async_copy(picks, picks_sm, local_sem.at[3])
        to_scalars.start()
        to_scalars.wait()
        for k in range(n_x):
            for j in range(per_x):
                text_xs[k, j] = text_y[picks_sm[0, k * per_x + j]]
        for k in range(1, n_x):
            start(hop_x(k))

    some(order[:4 * n_sect], send_q)

    @pl.when(lower)
    def _():
        for k in range(1, n_x):
            wait(hop_x(k))
        text_x[0] = text_xs[0]
        meta_x[0] = meta_xs[...]
        to_scalars = pltpu.make_async_copy(meta_x, meta_xm, local_sem.at[3])
        to_scalars.start()
        to_scalars.wait()
        for half, (text_to, meta_to) in enumerate(((text_own, meta_own), (text_far, meta_far))):
            lens = jnp.zeros((8, 128), jnp.int32)
            for j in range(REQ_G):
                at_x, count = jnp.int32(0), jnp.int32(0)
                for k in range(n_x):
                    here = meta_xm[k, 0, (k * n_hi + half) * REQ_G + j]
                    at_x = jnp.where(here > 0, k, at_x)
                    count = jnp.where(here > 0, here, count)
                text_to[j] = text_x[at_x, half * REQ_G + j]
                lens = jnp.where(lane == j, count, lens)
            meta_to[...] = lens
        pl.semaphore_wait(barrier, 1)
        start(hop_up())

    some(order[4 * n_sect:], send_q)

    @pl.when(upper)
    def _():
        for copy in hop_up():
            copy.wait_recv()

    to_scalars = pltpu.make_async_copy(meta_own, meta_own_sm, local_sem.at[4])
    to_scalars.start()
    to_scalars.wait()

    place = lax.broadcasted_iota(jnp.int32, (txt, HD), 0)
    spot_t = lax.broadcasted_iota(jnp.int32, (txt, HD), 1)
    for j in range(REQ_G):
        block, part = blocks + (j * txt) // tok, pl.ds((j * txt) % tok, txt)
        kv[block, 0, part] = text_own[j, 0]
        kv[block, 1, part] = text_own[j, 1]
        live = (spot_t == j) & (place < meta_own_sm[0, j])
        k_mask[block, part] = jnp.where((spot_t < REQ_G) & ~live, FAR, 0.0).astype(jnp.bfloat16)

    own_kv.wait()
    own_q.wait()
    each_peer(lambda d, c: move_kv(d, c).wait())

    factor = LOG2E / HD ** 0.5
    pair = n_sect * tok

    def attend(d):
        both = pl.ds(d * n_sect, n_sect)
        score[...] = lax.dot_general(
            jnp.concatenate([qb[both].reshape(pair, HD), q_mask[both].reshape(pair, HD)], axis=1),
            jnp.concatenate([kv[:, 0].reshape(keys, HD), k_mask[...].reshape(keys, HD)], axis=1),
            (((1,), (1,)), ((), ())), preferred_element_type=jnp.float32)
        top = jnp.max(score[...], axis=1, keepdims=True)
        prob[...] = jnp.exp2((score[...] - top) * factor).astype(jnp.bfloat16)
        mixed = jnp.dot(
            prob[...], jnp.concatenate([kv[:, 1].reshape(keys, HD), jnp.ones((keys, HD), jnp.bfloat16)], axis=1),
            preferred_element_type=jnp.float32)
        ob[both] = (mixed[:, :HD] / mixed[:, HD:]).astype(jnp.bfloat16).reshape(n_sect, tok, HD)

    for c in range(1, n_sect):
        move_q(0, c).wait()
    attend(0)
    for c in range(1, n_sect):
        move_o(0, c).start()

    @pl.loop(1, n_seq)
    def _(i):
        d = nth(i)
        for c in range(n_sect):
            move_q(d, c).wait()
        attend(d)
        for c in range(n_sect):
            move_o(d, c).start()

    @pl.when(lower)
    def _():
        for copy in hop_up():
            copy.wait_send()

    out_ref[:, columns(0, 0)] = ob[0]

    def finish(d, c):
        move_o(d, c).wait()
        out_ref[:, columns(d, c)] = landed[d * n_sect + c]

    each_peer(finish)


def local(mesh, qkv_img, img_seg, text_kv, txt_len, req_slot):
    n_seq, n_sect = mesh.shape["seq"], mesh.shape["sect"]
    n_hi, n_x, n_y = GRID
    blocks = n_seq * n_sect
    tok, width = qkv_img.shape[1], qkv_img.shape[3]
    txt = text_kv.shape[2]
    keys = blocks * tok + REQ_G * txt
    x = jnp.transpose(qkv_img[0], (1, 0, 2))
    dma = pltpu.SemaphoreType.DMA
    bf16, i32 = jnp.bfloat16, jnp.int32
    out = pl.pallas_call(
        functools.partial(kernel, (n_seq, n_sect, n_hi, n_x, n_y)),
        out_shape=jax.ShapeDtypeStruct((tok, width), bf16),
        in_specs=[
            pl.BlockSpec(memory_space=pl.ANY),
            pl.BlockSpec(memory_space=pl.ANY),
            pl.BlockSpec(memory_space=pl.ANY),
            pl.BlockSpec(memory_space=pl.ANY),
            pl.BlockSpec(memory_space=pl.ANY),
        ],
        out_specs=pl.BlockSpec(memory_space=pltpu.VMEM),
        scratch_shapes=[
            pltpu.VMEM((keys // tok, 2, tok, HD), bf16),
            pltpu.VMEM((keys // tok, tok, HD), bf16),
            pltpu.VMEM((blocks, tok, HD), bf16),
            pltpu.VMEM((blocks, tok, HD), bf16),
            pltpu.VMEM((blocks, tok, HD), bf16),
            pltpu.VMEM((blocks, tok, HD), bf16),
            pltpu.VMEM((n_sect * tok, keys), jnp.float32),
            pltpu.VMEM((n_sect * tok, keys), bf16),
            pltpu.VMEM((8, tok), i32),
            pltpu.VMEM((blocks, 8, tok), i32),
            pltpu.VMEM((REQ_G, 2, txt, HD), bf16),
            pltpu.VMEM((n_hi * n_y * REQ_G, 2, txt, HD), bf16),
            pltpu.VMEM((n_x, n_hi * REQ_G, 2, txt, HD), bf16),
            pltpu.VMEM((n_x, n_hi * REQ_G, 2, txt, HD), bf16),
            pltpu.VMEM((REQ_G, 2, txt, HD), bf16),
            pltpu.VMEM((REQ_G, 2, txt, HD), bf16),
            pltpu.VMEM((8, 128), i32),
            pltpu.VMEM((8, 128), i32),
            pltpu.VMEM((n_hi * n_y, 8, 128), i32),
            pltpu.VMEM((8, 128), i32),
            pltpu.VMEM((8, 128), i32),
            pltpu.VMEM((n_x, 8, 128), i32),
            pltpu.VMEM((8, 128), i32),
            pltpu.VMEM((8, 128), i32),
            pltpu.SMEM((n_hi * n_y, 8, 128), i32),
            pltpu.SMEM((8, 128), i32),
            pltpu.SMEM((n_x, 8, 128), i32),
            pltpu.SMEM((8, 128), i32),
            pltpu.SMEM((REQ_G,), i32),
            pltpu.SMEM((REQ_G,), i32),
            pltpu.VMEM((1, tok), i32),
            dma((8,)),
            dma((blocks,)), dma((blocks,)),
            dma((blocks,)), dma((blocks,)),
            dma((blocks,)), dma((blocks,)),
            dma((blocks,)), dma((blocks,)),
            dma((2,)), dma((2,)),
            dma((2,)), dma((2,)),
            dma((2, n_hi, n_y)), dma((2, n_hi, n_y)),
            dma((2, n_x)), dma((2, n_x)),
            dma((2,)), dma((2,)),
        ],
        compiler_params=pltpu.CompilerParams(
            collective_id=0, has_side_effects=True, vmem_limit_bytes=63 * 1024 * 1024),
        name="routed_attention",
    )(req_slot, txt_len, x, img_seg, text_kv)
    return out[None]


def solution(mesh):
    return jax.shard_map(
        functools.partial(local, mesh),
        mesh=mesh,
        in_specs=(
            P("grp", ("sect", "seq"), None, None),
            P("grp", ("sect", "seq")),
            P("grp", None, None, ("sect", "seq")),
            P("grp"),
            P("grp"),
        ),
        out_specs=P("grp", ("sect", "seq"), None),
        check_vma=False,
    )
```

time: 130 us -> 120 us (0.923)
  the two profiles are of different devices: /device:TPU:1 before, /device:TPU:385 now
where the time goes in v2:
time: 120 us
  Pallas kernels  118 us (98%)
  local copies, waits for them, and re-layouts  1.88 us (2%)
    pallas_call x1, Pallas kernels, local(): pl.pallas_call(functools.partial(kernel, (n_seq, n_sect, n_hi, n_x, n_y))...  118 us

profile of v2, /device:TPU:385, one launch (start us, length us, event | category | flops | bytes accessed | tf_op | source)
XLA Modules:
  0.0 119.5 jit_solution(276974315789914096)
XLA Ops:
  0.0 117.6 %routed_attention.1 = bf16[128,2048]{1,0:T(8,128)(2,1)} custom-call(s32[4]{0:T(128)} %slot_ref.1, s32[4]{0:T(128)} %len_ref.1, bf16[3,128,2048]{2,1,0:T(8,128)(2,1)} %bitcast.5, s32[1,128]{1,0:T(1,128)} %seg_ref.1, bf16[4,2,64,128]{3,2,1,0:T(8,128)(2,1)} %text_ref.1), custom_call_target="tpu_custom_call" | custom-call | tf_op jit(solution)/shard_map/routed_attention/pallas_call | solution.py:394
  117.6 1.9 %copy.7 = bf16[1,128,2048]{2,1,0:T(8,128)(2,1)} copy(bf16[1,128,2048]{2,1,0:T(8,128)(2,1)} %bitcast.4) | data formatting | bytes 1048576

commit v3 on v2

--- a/solution.py
+++ b/solution.py
@@ -10,6 +10,7 @@
 HD = 128
 REQ_G = 4
 GRID = (2, 4, 4)
+SPLIT = 3
 MESH = pl.DeviceIdType.MESH
 
 FAR = -2097152.0
@@ -24,8 +25,8 @@
     text_in, text_y, text_xs, text_x, text_far, text_own,
     meta_send, meta_in, meta_y, picks, meta_xs, meta_x, meta_far, meta_own,
     meta_sm, picks_sm, meta_xm, meta_own_sm, slots, counts, seg_row,
-    local_sem, seg_ss, seg_rs, kv_ss, kv_rs, q_ss, q_rs, o_ss, o_rs,
-    ta_s, ta_r, tb_s, tb_r, ty_s, ty_r, tx_s, tx_r, tc_s, tc_r,
+    local_sem, far_in, seg_ss, seg_rs, kv_ss, kv_rs, q_ss, q_rs, o_ss, o_rs,
+    ta_s, ta_r, tb_s, tb_r, td_s, td_r, ty_s, ty_r, tx_s, tx_r, tc_s, tc_r,
 ):
     n_seq, n_sect, n_hi, n_x, n_y = dims
     blocks = n_seq * n_sect
@@ -72,7 +73,7 @@
         return n_seq // 2 + (2 * (i % 2) - 1) * (i // 2) if isinstance(i, int) else (
             n_seq // 2 + (2 * lax.rem(i, 2) - 1) * lax.div(i, 2))
 
-    order = [(nth(i), c) for i in range(1, n_seq) for c in range(n_sect)] + [(0, c) for c in range(1, n_sect)]
+    order = [(d, c) for a, b in ((4, 3), (5, 2), (6, 1)) for c in range(n_sect) for d in (a, b)] + [(7, 0), (7, 1)] + [(0, c) for c in range(1, n_sect)]
 
     def some(places, body):
         for d, c in places:
@@ -108,6 +109,7 @@
             greet(along_y(k))
         for k in range(1, n_x):
             greet(along_x(k))
+        greet(far)
 
     for copy in small:
         copy.wait()
@@ -123,12 +125,11 @@
     @pl.when(lower)
     def _():
         pl.semaphore_wait(barrier, blocks - 1 + n_y - 1 + n_x - 1)
-        greet(far)
 
     @pl.when(upper)
     def _():
         pl.semaphore_wait(barrier, blocks - 1 + 1)
-        greet(far)
+        pl.semaphore_signal(far_in, inc=1, device_id=far, device_id_type=MESH)
 
     def remote(src, dst, ss, rs, device):
         return pltpu.make_async_remote_copy(
@@ -146,7 +147,9 @@
         mate = peer(n_seq - 1, 0)
         return (
             remote(meta_send, meta_in, ta_s.at[0], ta_r.at[0], mate),
-            remote(text_ref, text_in, ta_s.at[1], ta_r.at[1], mate),
+            remote(
+                text_ref.at[pl.ds(0, SPLIT)], text_in.at[pl.ds(0, SPLIT)],
+                ta_s.at[1], ta_r.at[1], mate),
         )
 
     def requests(half, k):
@@ -155,8 +158,20 @@
     def hop_down():
         return (
             remote(meta_in, meta_y.at[n_y], tb_s.at[0], tb_r.at[0], far),
-            remote(text_in, text_y.at[requests(1, 0)], tb_s.at[1], tb_r.at[1], far),
+            remote(
+                text_in.at[pl.ds(0, SPLIT)], text_y.at[pl.ds(n_y * REQ_G, SPLIT)],
+                tb_s.at[1], tb_r.at[1], far),
         )
+
+    late = pl.ds(SPLIT, REQ_G - SPLIT)
+
+    def hop_down_first():
+        return remote(text_ref.at[late], text_in.at[late], td_s.at[0], td_r.at[0], far)
+
+    def hop_mirror_last():
+        return remote(
+            text_in.at[late], text_y.at[pl.ds(n_y * REQ_G + SPLIT, REQ_G - SPLIT)],
+            td_s.at[1], td_r.at[1], peer(n_seq - 1, 0))
 
     def hop_y(half, k):
         meta_src = meta_y.at[n_y] if half else meta_send
@@ -205,15 +220,16 @@
     @pl.when(upper)
     def _():
         start(hop_mirror())
-
+        hop_down_first().start()
+
+    some(order[:n_sect], send_kv)
     each_peer(lambda d, c: move_seg(d, c).start())
+    some(order[n_sect:n1], send_kv)
 
     @pl.when(lower)
     def _():
         for k in range(1, n_y):
             start(hop_y(0, k))
-
-    some(order[:n1], send_kv)
 
     own_text = pltpu.make_async_copy(text_ref, text_y.at[requests(0, 0)], local_sem.at[0])
     own_text.start()
@@ -227,6 +243,12 @@
     def _():
         wait(hop_mirror())
         start(hop_down())
+        hop_down_first().wait_send()
+
+    @pl.when(lower)
+    def _():
+        hop_down_first().wait_recv()
+        hop_mirror_last().start()
 
     some(order[n1:n2], send_kv)
 
@@ -246,6 +268,7 @@
     def _():
         for copy in hop_down():
             copy.wait_recv()
+        hop_mirror_last().wait()
         for k in range(1, n_y):
             start(hop_y(1, k))
 
@@ -309,7 +332,7 @@
                 text_to[j] = text_x[at_x, half * REQ_G + j]
                 lens = jnp.where(lane == j, count, lens)
             meta_to[...] = lens
-        pl.semaphore_wait(barrier, 1)
+        pl.semaphore_wait(far_in, 1)
         start(hop_up())
 
     some(order[4 * n_sect:], send_q)
@@ -435,10 +458,12 @@
             pltpu.SMEM((REQ_G,), i32),
             pltpu.VMEM((1, tok), i32),
             dma((8,)),
+            pltpu.SemaphoreType.REGULAR,
             dma((blocks,)), dma((blocks,)),
             dma((blocks,)), dma((blocks,)),
             dma((blocks,)), dma((blocks,)),
             dma((blocks,)), dma((blocks,)),
+            dma((2,)), dma((2,)),
             dma((2,)), dma((2,)),
             dma((2,)), dma((2,)),
             dma((2, n_hi, n_y)), dma((2, n_hi, n_y)),

time: 120 us -> 113 us (0.942)
  the two profiles are of different devices: /device:TPU:385 before, /device:TPU:1 now
where the time goes in v3:
time: 113 us
  Pallas kernels  111 us (98%)
  local copies, waits for them, and re-layouts  1.88 us (2%)
    pallas_call x1, Pallas kernels, local(): pl.pallas_call(functools.partial(kernel, (n_seq, n_sect, n_hi, n_x, n_y))...  111 us

profile of v3, /device:TPU:1, one launch (start us, length us, event | category | flops | bytes accessed | tf_op | source)
XLA Modules:
  0.0 112.8 jit_solution(10878293462582057204)
XLA Ops:
  0.0 110.9 %routed_attention.1 = bf16[128,2048]{1,0:T(8,128)(2,1)} custom-call(s32[4]{0:T(128)} %slot_ref.1, s32[4]{0:T(128)} %len_ref.1, bf16[3,128,2048]{2,1,0:T(8,128)(2,1)} %bitcast.5, s32[1,128]{1,0:T(1,128)} %seg_ref.1, bf16[4,2,64,128]{3,2,1,0:T(8,128)(2,1)} %text_ref.1), custom_call_target="tpu_custom_call" | custom-call | tf_op jit(solution)/shard_map/routed_attention/pallas_call | solution.py:417
  111.0 1.9 %copy.7 = bf16[1,128,2048]{2,1,0:T(8,128)(2,1)} copy(bf16[1,128,2048]{2,1,0:T(8,128)(2,1)} %bitcast.4) | data formatting | bytes 1048576

commit v4 on v3

--- a/solution.py
+++ b/solution.py
@@ -25,7 +25,7 @@
     text_in, text_y, text_xs, text_x, text_far, text_own,
     meta_send, meta_in, meta_y, picks, meta_xs, meta_x, meta_far, meta_own,
     meta_sm, picks_sm, meta_xm, meta_own_sm, slots, counts, seg_row,
-    local_sem, far_in, seg_ss, seg_rs, kv_ss, kv_rs, q_ss, q_rs, o_ss, o_rs,
+    local_sem, far_in, rounds, seg_ss, seg_rs, kv_ss, kv_rs, q_ss, q_rs, o_ss, o_rs,
     ta_s, ta_r, tb_s, tb_r, td_s, td_r, ty_s, ty_r, tx_s, tx_r, tc_s, tc_r,
 ):
     n_seq, n_sect, n_hi, n_x, n_y = dims
@@ -101,7 +101,8 @@
     def greet(device):
         pl.semaphore_signal(barrier, inc=1, device_id=device, device_id_type=MESH)
 
-    each_peer(lambda d, c: greet(peer(d, c)))
+    near = [(n_seq - 1, 0), (0, 1)] + [(1 << b, 0) for b in range(n_seq.bit_length() - 2)]
+    some(near, lambda d, c: greet(peer(d, c)))
 
     @pl.when(lower)
     def _():
@@ -124,11 +125,11 @@
 
     @pl.when(lower)
     def _():
-        pl.semaphore_wait(barrier, blocks - 1 + n_y - 1 + n_x - 1)
+        pl.semaphore_wait(barrier, len(near) + n_y - 1 + n_x - 1)
 
     @pl.when(upper)
     def _():
-        pl.semaphore_wait(barrier, blocks - 1 + 1)
+        pl.semaphore_wait(barrier, len(near) + 1)
         pl.semaphore_signal(far_in, inc=1, device_id=far, device_id_type=MESH)
 
     def remote(src, dst, ss, rs, device):
@@ -215,12 +216,19 @@
     def send_q(d, c):
         move_q(d, c).start()
 
-    n1, n2 = 2 * n_sect, 5 * n_sect
+    n1, n2 = 2 * n_sect - 1, 5 * n_sect - 1
 
     @pl.when(upper)
     def _():
         start(hop_mirror())
         hop_down_first().start()
+
+    some(near[:1], send_kv)
+    for r, (d, c) in enumerate(near[1:]):
+        pl.semaphore_signal(rounds.at[r], inc=1, device_id=peer(d, c), device_id_type=MESH)
+        pl.semaphore_wait(rounds.at[r], 1)
+    q_order = order
+    order = [place for place in order if place not in near[:1]]
 
     some(order[:n_sect], send_kv)
     each_peer(lambda d, c: move_seg(d, c).start())
@@ -310,7 +318,7 @@
         for k in range(1, n_x):
             start(hop_x(k))
 
-    some(order[:4 * n_sect], send_q)
+    some(q_order[:4 * n_sect], send_q)
 
     @pl.when(lower)
     def _():
@@ -335,7 +343,7 @@
         pl.semaphore_wait(far_in, 1)
         start(hop_up())
 
-    some(order[4 * n_sect:], send_q)
+    some(q_order[4 * n_sect:], send_q)
 
     @pl.when(upper)
     def _():
@@ -375,21 +383,21 @@
             preferred_element_type=jnp.float32)
         ob[both] = (mixed[:, :HD] / mixed[:, HD:]).astype(jnp.bfloat16).reshape(n_sect, tok, HD)
 
-    for c in range(1, n_sect):
-        move_q(0, c).wait()
-    attend(0)
-    for c in range(1, n_sect):
-        move_o(0, c).start()
-
     @pl.loop(1, n_seq)
     def _(i):
         d = nth(i)
         for c in range(n_sect):
-            move_q(d, c).wait()
+            move_q(d, c).wait_recv()
         attend(d)
         for c in range(n_sect):
             move_o(d, c).start()
 
+    for c in range(1, n_sect):
+        move_q(0, c).wait_recv()
+    attend(0)
+    for c in range(1, n_sect):
+        move_o(0, c).start()
+
     @pl.when(lower)
     def _():
         for copy in hop_up():
@@ -398,6 +406,7 @@
     out_ref[:, columns(0, 0)] = ob[0]
 
     def finish(d, c):
+        move_q(d, c).wait_send()
         move_o(d, c).wait()
         out_ref[:, columns(d, c)] = landed[d * n_sect + c]
 
@@ -459,6 +468,7 @@
             pltpu.VMEM((1, tok), i32),
             dma((8,)),
             pltpu.SemaphoreType.REGULAR,
+            pltpu.SemaphoreType.REGULAR((3,)),
             dma((blocks,)), dma((blocks,)),
             dma((blocks,)), dma((blocks,)),
             dma((blocks,)), dma((blocks,)),

time: 113 us -> 113 us (level)
  no operation moved by 1% of the time
where the time goes in v4:
time: 113 us
  Pallas kernels  111 us (98%)
  local copies, waits for them, and re-layouts  1.88 us (2%)
    pallas_call x1, Pallas kernels, local(): pl.pallas_call(functools.partial(kernel, (n_seq, n_sect, n_hi, n_x, n_y))...  111 us

profile of v4, /device:TPU:1, one launch (start us, length us, event | category | flops | bytes accessed | tf_op | source)
XLA Modules:
  0.0 113.2 jit_solution(7066291126571176881)
XLA Ops:
  0.0 111.4 %routed_attention.1 = bf16[128,2048]{1,0:T(8,128)(2,1)} custom-call(s32[4]{0:T(128)} %slot_ref.1, s32[4]{0:T(128)} %len_ref.1, bf16[3,128,2048]{2,1,0:T(8,128)(2,1)} %bitcast.5, s32[1,128]{1,0:T(1,128)} %seg_ref.1, bf16[4,2,64,128]{3,2,1,0:T(8,128)(2,1)} %text_ref.1), custom_call_target="tpu_custom_call" | custom-call | tf_op jit(solution)/shard_map/routed_attention/pallas_call | solution.py:426
  111.4 1.9 %copy.7 = bf16[1,128,2048]{2,1,0:T(8,128)(2,1)} copy(bf16[1,128,2048]{2,1,0:T(8,128)(2,1)} %bitcast.4) | data formatting | bytes 1048576

commit v5 on v4

--- a/solution.py
+++ b/solution.py
@@ -10,7 +10,7 @@
 HD = 128
 REQ_G = 4
 GRID = (2, 4, 4)
-SPLIT = 3
+SPLIT = 4
 MESH = pl.DeviceIdType.MESH
 
 FAR = -2097152.0
@@ -26,7 +26,7 @@
     meta_send, meta_in, meta_y, picks, meta_xs, meta_x, meta_far, meta_own,
     meta_sm, picks_sm, meta_xm, meta_own_sm, slots, counts, seg_row,
     local_sem, far_in, rounds, seg_ss, seg_rs, kv_ss, kv_rs, q_ss, q_rs, o_ss, o_rs,
-    ta_s, ta_r, tb_s, tb_r, td_s, td_r, ty_s, ty_r, tx_s, tx_r, tc_s, tc_r,
+    ta_s, ta_r, tb_s, tb_r, ty_s, ty_r, tx_s, tx_r, tc_s, tc_r,
 ):
     n_seq, n_sect, n_hi, n_x, n_y = dims
     blocks = n_seq * n_sect
@@ -164,16 +164,6 @@
                 tb_s.at[1], tb_r.at[1], far),
         )
 
-    late = pl.ds(SPLIT, REQ_G - SPLIT)
-
-    def hop_down_first():
-        return remote(text_ref.at[late], text_in.at[late], td_s.at[0], td_r.at[0], far)
-
-    def hop_mirror_last():
-        return remote(
-            text_in.at[late], text_y.at[pl.ds(n_y * REQ_G + SPLIT, REQ_G - SPLIT)],
-            td_s.at[1], td_r.at[1], peer(n_seq - 1, 0))
-
     def hop_y(half, k):
         meta_src = meta_y.at[n_y] if half else meta_send
         text_src = text_y.at[requests(1, 0)] if half else text_ref
@@ -221,7 +211,6 @@
     @pl.when(upper)
     def _():
         start(hop_mirror())
-        hop_down_first().start()
 
     some(near[:1], send_kv)
     for r, (d, c) in enumerate(near[1:]):
@@ -251,12 +240,6 @@
     def _():
         wait(hop_mirror())
         start(hop_down())
-        hop_down_first().wait_send()
-
-    @pl.when(lower)
-    def _():
-        hop_down_first().wait_recv()
-        hop_mirror_last().start()
 
     some(order[n1:n2], send_kv)
 
@@ -276,7 +259,6 @@
     def _():
         for copy in hop_down():
             copy.wait_recv()
-        hop_mirror_last().wait()
         for k in range(1, n_y):
             start(hop_y(1, k))
 
@@ -475,7 +457,6 @@
             dma((blocks,)), dma((blocks,)),
             dma((2,)), dma((2,)),
             dma((2,)), dma((2,)),
-            dma((2,)), dma((2,)),
             dma((2, n_hi, n_y)), dma((2, n_hi, n_y)),
             dma((2, n_x)), dma((2, n_x)),
             dma((2,)), dma((2,)),

time: 113 us -> 114 us (level)
  the two profiles are of different devices: /device:TPU:1 before, /device:TPU:415 now
where the time goes in v5:
time: 114 us
  Pallas kernels  112 us (98%)
  local copies, waits for them, and re-layouts  1.88 us (2%)
    pallas_call x1, Pallas kernels, local(): pl.pallas_call(functools.partial(kernel, (n_seq, n_sect, n_hi, n_x, n_y))...  112 us

profile of v5, /device:TPU:415, one launch (start us, length us, event | category | flops | bytes accessed | tf_op | source)
XLA Modules:
  0.0 114.1 jit_solution(5733483723167330599)
XLA Ops:
  0.0 112.2 %routed_attention.1 = bf16[128,2048]{1,0:T(8,128)(2,1)} custom-call(s32[4]{0:T(128)} %slot_ref.1, s32[4]{0:T(128)} %len_ref.1, bf16[3,128,2048]{2,1,0:T(8,128)(2,1)} %bitcast.5, s32[1,128]{1,0:T(1,128)} %seg_ref.1, bf16[4,2,64,128]{3,2,1,0:T(8,128)(2,1)} %text_ref.1), custom_call_target="tpu_custom_call" | custom-call | tf_op jit(solution)/shard_map/routed_attention/pallas_call | solution.py:408
  112.2 1.9 %copy.7 = bf16[1,128,2048]{2,1,0:T(8,128)(2,1)} copy(bf16[1,128,2048]{2,1,0:T(8,128)(2,1)} %bitcast.4) | data formatting | bytes 1048576
